TPU v7x, 512 devices: a whole 4x8x8 slice. The times are simulated.
512 devices in a mesh: grp: 16 (over y, z_lo), row: 32 (over z_hi, x, core).
Axes of the slice: x: 4, y: 8, z: 8 (z_hi: 4, z_lo: 2; z = z_hi * 2 + z_lo), core: 2. Of those that a mesh axis runs over, the one named last changes fastest.
Arguments:
- cov_prior: float32 [16384, 16384], P(('grp', 'row')), may hold values from -7 to 23, as said below
- courant_x_field: float32 [128, 128], replicated, may hold values from -0.35 to 0.35
- courant_y_field: float32 [128, 128], replicated, may hold values from -0.35 to 0.35
- obs_cells: int32 [2, 128], replicated, may hold values from 0 to 16383
- obs_var: float32 [2, 128], replicated, may hold values from 0.5 to 2
Outputs:
- analysis: float32 [16384, 16384], P('grp', 'row')
Inputs may be any that keep to these rules, and one draw needn't show every extreme that they name: `cov_prior`: symmetric and positive definite. `obs_cells`: a cell may be observed more than once in an update.
All inputs are finite; a program needn't handle non-finite values.
Results may differ from a plain program's by a relative error of at most 0.0002.
Values sent between devices are 32-bit elements; how exact they have to be, the bound alone decides.
A program may use at most 64 MiB of HBM per device.

v0:
```python
import jax
import jax.numpy as jnp
from jax import lax
from jax.sharding import PartitionSpec as P

ZONAL_POINTS = 128
NY = 128
NCELL = 16384
UPDATES = 2
diffusion = 0.1


def extended_2(block, sides, width):
    for axis, dim in sides:
        count = lax.axis_size(axis)
        forward = [(i, i + 1) for i in range(count - 1)]
        backward = [(target, source) for source, target in forward]
        low = lax.ppermute(
            lax.slice_in_dim(block, block.shape[dim] - width, None, axis=dim), axis, forward
        )
        high = lax.ppermute(lax.slice_in_dim(block, 0, width, axis=dim), axis, backward)
        block = jnp.concatenate([low, block, high], axis=dim)
    return block


def tendency_first(padded, u_part, v_part):
    middle = padded[:, 2:-2]
    center = middle[:, :, 2:-2]
    along_x = (
        8.0 * (middle[:, :, 3:-1] - middle[:, :, 1:-3]) - (middle[:, :, 4:] - middle[:, :, :-4])
    ) / 12.0
    column = padded[:, :, 2:-2]
    along_y = (8.0 * (column[:, 3:-1] - column[:, 1:-3]) - (column[:, 4:] - column[:, :-4])) / 12.0
    laplace = (
        middle[:, :, 3:-1] + middle[:, :, 1:-3] + column[:, 3:-1] + column[:, 1:-3] - 4.0 * center
    )
    return diffusion * laplace - u_part * along_x - v_part * along_y


def heun_whole(fields, courant_x_field, courant_y_field):
    slope_first = tendency_first(
        jnp.pad(fields, ((0, 0), (2, 2), (2, 2))), courant_x_field, courant_y_field
    )
    latter_increment = tendency_first(
        jnp.pad(fields + slope_first, ((0, 0), (2, 2), (2, 2))), courant_x_field, courant_y_field
    )
    return fields + 0.5 * (slope_first + latter_increment)


def tendency_last(extended, u_part, v_part):
    padded = jnp.pad(extended, ((0, 0), (2, 2), (0, 0)))
    middle = padded[2:-2]
    center = middle[:, 2:-2]
    along_x = (8.0 * (middle[:, 3:-1] - middle[:, 1:-3]) - (middle[:, 4:] - middle[:, :-4])) / 12.0
    column = padded[:, 2:-2]
    along_y = (8.0 * (column[3:-1] - column[1:-3]) - (column[4:] - column[:-4])) / 12.0
    laplace = middle[:, 3:-1] + middle[:, 1:-3] + column[3:-1] + column[1:-3] - 4.0 * center
    return diffusion * laplace - u_part * along_x - v_part * along_y


def linear_source_term(local_block, courant_x_field, courant_y_field):
    meridional_count = local_block.shape[0]
    first_row = lax.axis_index("grp") * meridional_count
    u_padded = jnp.pad(courant_x_field, ((4, 4), (0, 0)))
    v_padded = jnp.pad(courant_y_field, ((4, 4), (0, 0)))
    u_inner = lax.dynamic_slice_in_dim(u_padded, first_row + 4, meridional_count, 0)[:, :, None]
    v_inner = lax.dynamic_slice_in_dim(v_padded, first_row + 4, meridional_count, 0)[:, :, None]

    def section_slope(current):
        extended = extended_2(current, (("grp", 0),), 2)
        return tendency_last(extended, u_inner, v_inner)

    slope_first = section_slope(local_block)
    latter_increment = section_slope(local_block + slope_first)
    local_block = local_block + 0.5 * (slope_first + latter_increment)
    return local_block


def local(cov_prior, courant_x_field, courant_y_field, obs_cells, obs_var):
    row_count = cov_prior.shape[0]
    fields = cov_prior.reshape(row_count, NY, ZONAL_POINTS)
    fields = heun_whole(fields, courant_x_field, courant_y_field)
    advanced = fields.reshape(row_count, NCELL)
    members = lax.axis_size("row")
    zonal_extent = NCELL // members
    meridional_count = row_count * members // ZONAL_POINTS
    arrived_value = lax.all_to_all(advanced, "row", split_axis=1, concat_axis=0, tiled=True)
    predicted_tracer = linear_source_term(
        arrived_value.reshape(meridional_count, ZONAL_POINTS, zonal_extent),
        courant_x_field,
        courant_y_field,
    )
    posterior_mean = predicted_tracer.reshape(meridional_count * ZONAL_POINTS, zonal_extent)
    local_rows = posterior_mean.shape[0]
    first_cell = lax.axis_index("grp") * local_rows
    first_column = lax.axis_index("row") * zonal_extent
    for update_number in range(UPDATES):
        picked = obs_cells[update_number]
        row_offset = picked - first_cell
        row_owned = (row_offset >= 0) & (row_offset < local_rows)
        rows_part = jnp.where(
            row_owned[:, None], posterior_mean[jnp.clip(row_offset, 0, local_rows - 1)], 0.0
        )
        observed_rows = lax.psum(rows_part, "grp")
        column_offset = picked - first_column
        column_owned = (column_offset >= 0) & (column_offset < zonal_extent)
        safe_column = jnp.clip(column_offset, 0, zonal_extent - 1)
        cols_part = jnp.where(column_owned[None, :], posterior_mean[:, safe_column], 0.0)
        inner_part = jnp.where(column_owned[None, :], observed_rows[:, safe_column], 0.0)
        observed_cols, inner_block = lax.psum((cols_part, inner_part), "row")
        system = 0.5 * (inner_block + inner_block.T) + jnp.diag(obs_var[update_number])
        factor = jnp.linalg.cholesky(system)
        halfway = lax.linalg.triangular_solve(factor, observed_rows, left_side=True, lower=True)
        weights = lax.linalg.triangular_solve(
            factor, halfway, left_side=True, lower=True, transpose_a=True
        )
        posterior_mean = posterior_mean - jnp.dot(
            observed_cols, weights, precision=lax.Precision.HIGHEST
        )
    return posterior_mean


def solution(mesh):
    placed = (P(("grp", "row"), None), P(), P(), P(), P())
    return jax.shard_map(
        local, mesh=mesh, in_specs=placed, out_specs=P("grp", "row"), check_vma=False
    )
```

profile of v0, /device:TPU:8, one launch (start us, length us, event | category | flops | bytes accessed | tf_op | source)
XLA Modules:
  0.0 1064.2 jit_solution(17766533963469429662)
XLA Ops:
  6.5 2.0 copy.29
  8.6 2.6 bitcast_add_fusion.4
  11.2 4.0 fusion.20
  18.1 54.5 %all_to_all.16 = f32[32,32,512]{2,0,1:T(8,128)S(1)} all-to-all(f32[32,32,512]{2,0,1:T(8,128)S(1)} %copy.6), channel_id=1, replica_groups=mesh['grp'=16,'row'=32] {'row'}, dimensions={1} | all-to-all | bytes 4194304 | tf_op jit(solution)/shard_map/all_to_all | solution.py:87
  73.6 14.2 %collective-permute-start = (f32[2,128,512]{2,1,0:T(8,128)}, f32[2,128,512]{2,1,0:T(8,128)S(1)}, u32[]{:S(2)}, u32[]{:S(2)}) collective-permute-start(f32[2,128,512]{2,1,0:T(8,128)} %bitcast.2), channel_id=1, source_target_pairs={{0,32},{32,64},{64,96},{96,128},{128,160},{160,192},{192,224},{224... | collective-permute-start | bytes 1572872 | tf_op jit(solution)/shard_map/ppermute | solution.py:18
  89.8 20.8 %collective-permute-done = f32[2,128,512]{2,1,0:T(8,128)S(1)} collective-permute-done((f32[2,128,512]{2,1,0:T(8,128)}, f32[2,128,512]{2,1,0:T(8,128)S(1)}, u32[]{:S(2)}, u32[]{:S(2)}) %collective-permute-start) | collective-permute-done | bytes 524320 | tf_op jit(solution)/shard_map/ppermute | solution.py:18
  113.6 3.8 collective-permute-start.2
  117.4 3.0 collective-permute-start.3
  120.4 18.5 %collective-permute-done.2 = f32[2,128,512]{2,1,0:T(8,128)S(1)} collective-permute-done((f32[2,128,512]{2,1,0:T(8,128)S(1)}, f32[2,128,512]{2,1,0:T(8,128)S(1)}, u32[]{:S(2)}, u32[]{:S(2)}) %collective-permute-start.2) | collective-permute-done | bytes 524320 | tf_op jit(solution)/shard_map/ppermute | solution.py:18
  138.9 2.5 collective-permute-done.3
  142.1 2.9 fusion.30
  145.0 2.6 gather_fusion.1
  150.3 2.6 gather_fusion
  153.9 131.3 %all-reduce.13.cloned.1.call-done = f32[128,512]{1,0:T(8,128)} async-done(((f32[128,512]{1,0:T(8,128)}), f32[128,512]{1,0:T(8,128)}) %all-reduce.13.cloned.1.call-update) | async-done | bytes 262160 | tf_op jit(solution)/shard_map/psum | solution.py:104
  288.1 284.4 %all-reduce.19.cloned.1.call-done = (f32[1024,128]{0,1:T(8,128)}, f32[128,128]{0,1:T(8,128)}) async-done(((f32[1024,128]{0,1:T(8,128)}, f32[128,128]{0,1:T(8,128)}), (f32[1024,128]{0,1:T(8,128)}, f32[128,128]{0,1:T(8,128)})) %all-reduce.19.cloned.1.call-update) | async-done | bytes 589840 | tf_op jit(solution)/shard_map/psum | solution.py:110
  574.6 11.7 %cholesky.44 = f32[128,128]{1,0:T(8,128)S(1)} custom-call(f32[128,128]{1,0:T(8,128)S(1)} %copy.13), custom_call_target="Cholesky" | custom-call | tf_op jit(solution)/shard_map/jit(cholesky)/cholesky | solution.py:112
  587.6 9.8 custom-call.11
  598.2 3.4 convolution_subtract_fusion.1
  605.3 2.6 gather_fusion.3
  608.9 132.8 %all-reduce.15.cloned.1.call-done = f32[128,512]{1,0:T(8,128)} async-done(((f32[128,512]{1,0:T(8,128)}), f32[128,512]{1,0:T(8,128)}) %all-reduce.15.cloned.1.call-update) | async-done | bytes 262160 | tf_op jit(solution)/shard_map/psum | solution.py:104
  744.3 284.4 %all-reduce.17.cloned.1.call-done = (f32[1024,128]{0,1:T(8,128)}, f32[128,128]{1,0:T(8,128)}) async-done(((f32[1024,128]{0,1:T(8,128)}, f32[128,128]{1,0:T(8,128)}), (f32[1024,128]{0,1:T(8,128)}, f32[128,128]{1,0:T(8,128)})) %all-reduce.17.cloned.1.call-update) | async-done | bytes 589840 | tf_op jit(solution)/shard_map/psum | solution.py:110
  1030.8 11.7 %cholesky.55 = f32[128,128]{1,0:T(8,128)S(1)} custom-call(f32[128,128]{1,0:T(8,128)S(1)} %fusion.47), custom_call_target="Cholesky" | custom-call | tf_op jit(solution)/shard_map/jit(cholesky)/cholesky | solution.py:112
  1043.9 9.8 custom-call.13
  1054.5 3.2 convolution_subtract_fusion
  (81 shorter events, 31.5 us)
Async XLA Ops:
  6.5 278.7 %all-reduce.13.cloned.1.call-start = ((), (), s32[]{:S(2)}) async-start(), calls=%async_computation.1 | async-start | bytes 524288 | tf_op jit(solution)/shard_map/psum | solution.py:104
  6.5 2.0 copy-start.5
  6.5 2.0 copy-start.6
  73.6 37.0 %collective-permute-start = (f32[2,128,512]{2,1,0:T(8,128)}, f32[2,128,512]{2,1,0:T(8,128)S(1)}, u32[]{:S(2)}, u32[]{:S(2)}) collective-permute-start(f32[2,128,512]{2,1,0:T(8,128)} %bitcast.2), channel_id=1, source_target_pairs={{0,32},{32,64},{64,96},{96,128},{128,160},{160,192},{192,224},{224... | collective-permute-start | bytes 1572872 | tf_op jit(solution)/shard_map/ppermute | solution.py:18
  87.8 23.3 %collective-permute-start.1 = (f32[2,128,512]{2,1,0:T(8,128)}, f32[2,128,512]{2,1,0:T(8,128)S(1)}, u32[]{:S(2)}, u32[]{:S(2)}) collective-permute-start(f32[2,128,512]{2,1,0:T(8,128)} %bitcast.4), channel_id=1, source_target_pairs={{32,0},{64,32},{96,64},{128,96},{160,128},{192,160},{224,192},{256... | collective-permute-start | bytes 1572872 | tf_op jit(solution)/shard_map/ppermute | solution.py:21
  113.5 6.8 copy-start.7
  113.6 25.3 %collective-permute-start.2 = (f32[2,128,512]{2,1,0:T(8,128)S(1)}, f32[2,128,512]{2,1,0:T(8,128)S(1)}, u32[]{:S(2)}, u32[]{:S(2)}) collective-permute-start(f32[2,128,512]{2,1,0:T(8,128)S(1)} %get-tuple-element.17), channel_id=1, source_target_pairs={{0,32},{32,64},{64,96},{96,128},{128,160},{160,192},{192,224},{224... | collective-permute-start | bytes 1572872 | tf_op jit(solution)/shard_map/ppermute | solution.py:18
  117.4 24.1 %collective-permute-start.3 = (f32[2,128,512]{2,1,0:T(8,128)S(1)}, f32[2,128,512]{2,1,0:T(8,128)S(1)}, u32[]{:S(2)}, u32[]{:S(2)}) collective-permute-start(f32[2,128,512]{2,1,0:T(8,128)S(1)} %get-tuple-element.16), channel_id=1, source_target_pairs={{32,0},{64,32},{96,64},{128,96},{160,128},{192,160},{224,192},{256... | collective-permute-start | bytes 1572872 | tf_op jit(solution)/shard_map/ppermute | solution.py:21
  145.0 3.5 copy-start
  148.4 424.1 %all-reduce.19.cloned.1.call-start = ((), (), s32[]{:S(2)}) async-start(), calls=%async_computation.4 | async-start | bytes 1179648 | tf_op jit(solution)/shard_map/psum | solution.py:110
  153.0 135.1 %copy-start.8 = (f32[2,128]{1,0:T(2,128)S(1)}, f32[2,128]{1,0:T(2,128)}, u32[]{:S(2)}) copy-start(f32[2,128]{1,0:T(2,128)} %param.14) | copy-start | bytes 3076
  285.3 312.1 %copy-start.2 = (f32[128,512]{1,0:T(8,128)S(1)}, f32[128,512]{1,0:T(8,128)}, u32[]{:S(2)}) copy-start(f32[128,512]{1,0:T(8,128)} %all-reduce.13.cloned.1.call-done) | copy-start | bytes 786436
  287.8 453.8 %all-reduce.15.cloned.1.call-start = ((), (), s32[]{:S(2)}) async-start(), calls=%async_computation.2 | async-start | bytes 524288 | tf_op jit(solution)/shard_map/psum | solution.py:104
  572.5 25.7 %copy-start.3 = (f32[1024,128]{0,1:T(8,128)S(1)}, f32[1024,128]{0,1:T(8,128)}, u32[]{:S(2)}) copy-start(f32[1024,128]{0,1:T(8,128)} %get-tuple-element.10) | copy-start | bytes 1572868
  603.2 425.5 %all-reduce.17.cloned.1.call-start = ((), (), s32[]{:S(2)}) async-start(), calls=%async_computation.3 | async-start | bytes 1179648 | tf_op jit(solution)/shard_map/psum | solution.py:110
  741.6 312.1 %copy-start.1 = (f32[128,512]{1,0:T(8,128)S(1)}, f32[128,512]{1,0:T(8,128)}, u32[]{:S(2)}) copy-start(f32[128,512]{1,0:T(8,128)} %all-reduce.15.cloned.1.call-done) | copy-start | bytes 786436
  1028.8 25.8 %copy-start.4 = (f32[1024,128]{0,1:T(8,128)S(1)}, f32[1024,128]{0,1:T(8,128)}, u32[]{:S(2)}) copy-start(f32[1024,128]{0,1:T(8,128)} %get-tuple-element.6) | copy-start | bytes 1572868
Sparse Core Ops, SparseCore 0:
  148.6 136.6 all-reduce.12
  288.5 283.9 all-reduce.18
  603.4 138.2 all-reduce.14
  744.8 283.9 all-reduce.16
where the time goes:
time: 1060 us
  waiting for transfers between devices  875 us (83%)
  other arithmetic  64.7 us (6%)
  blocking collectives  54.5 us (5%)
  local copies, waits for them, and re-layouts  24.5 us (2%)
  starting transfers between devices  23.4 us (2%)
  between operations  13.6 us (1%)
    psum x2, waiting for transfers between devices, local(): observed_cols, inner_block = lax.psum((cols_part, inner_part), 'row')  569 us
    psum x2, waiting for transfers between devices, local(): observed_rows = lax.psum(rows_part, 'grp')  264 us
    all_to_all x1, blocking collectives, local(): lax.all_to_all(advanced, 'row', split_axis=1, concat_axis=0, tiled=True)  54.5 us
    ppermute x2, waiting for transfers between devices, extended_2(): lax.ppermute(lax.slice_in_dim(block, block.shape[dim] - width, None, axis...  39.3 us
    another operation x7, other arithmetic, local(): factor = jnp.linalg.cholesky(system)  24.8 us
  transfers between devices with their start and end apart: 8, of which 8 were waited for; matrix products, arithmetic and copies ran while one was open for 1% of the time, Pallas kernels for 0%

commit v1 on v0

--- a/solution.py
+++ b/solution.py
@@ -101,7 +101,13 @@
         rows_part = jnp.where(
             row_owned[:, None], posterior_mean[jnp.clip(row_offset, 0, local_rows - 1)], 0.0
         )
-        observed_rows = lax.psum(rows_part, "grp")
+
+        def shape_the_run(array_in):
+            v_now = lax.all_gather(array_in, "grp")
+            state_now = jnp.sum(v_now, axis=0)
+            return state_now
+
+        observed_rows = shape_the_run(rows_part)
         column_offset = picked - first_column
         column_owned = (column_offset >= 0) & (column_offset < zonal_extent)
         safe_column = jnp.clip(column_offset, 0, zonal_extent - 1)

time: 1060 us -> 991 us (0.935)
  waiting for transfers between devices: 875 us -> 799 us
    psum x2 -> x0, waiting for transfers between devices: 264 us -> none  [local(): observed_rows = lax.psum(rows_part, 'grp')]
    all_gather x0 -> x2, waiting for transfers between devices: none -> 190 us  [shape_the_run(): v_now = lax.all_gather(array_in, 'grp')]
where the time goes in v1:
time: 991 us
  waiting for transfers between devices  799 us (81%)
  other arithmetic  70.1 us (7%)
  blocking collectives  54.5 us (5%)
  starting transfers between devices  23.4 us (2%)
  local copies, waits for them, and re-layouts  22.5 us (2%)
  between operations  13.6 us (1%)
    psum x2, waiting for transfers between devices, local(): observed_cols, inner_block = lax.psum((cols_part, inner_part), 'row')  567 us
    all_gather x2, waiting for transfers between devices, shape_the_run(): v_now = lax.all_gather(array_in, 'grp')  190 us
    all_to_all x1, blocking collectives, local(): lax.all_to_all(advanced, 'row', split_axis=1, concat_axis=0, tiled=True)  54.5 us
    ppermute x2, waiting for transfers between devices, extended_2(): lax.ppermute(lax.slice_in_dim(block, block.shape[dim] - width, None, axis...  39.3 us
    another operation x7, other arithmetic, local(): factor = jnp.linalg.cholesky(system)  24.8 us
    another operation x4, other arithmetic, local(): lax.linalg.triangular_solve(factor, halfway, left_side=True, lower=True,...  20.9 us
  transfers between devices with their start and end apart: 8, of which 8 were waited for; matrix products, arithmetic and copies ran while one was open for 1% of the time, Pallas kernels for 0%

profile of v1, /device:TPU:8, one launch (start us, length us, event | category | flops | bytes accessed | tf_op | source)
XLA Modules:
  0.0 990.7 jit_solution(4874920588327979472)
XLA Ops:
  8.6 2.6 bitcast_add_fusion.4
  11.2 4.0 fusion.20
  18.1 54.5 %all_to_all.16 = f32[32,32,512]{2,0,1:T(8,128)S(1)} all-to-all(f32[32,32,512]{2,0,1:T(8,128)S(1)} %copy.19), channel_id=1, replica_groups=mesh['grp'=16,'row'=32] {'row'}, dimensions={1} | all-to-all | bytes 4194304 | tf_op jit(solution)/shard_map/all_to_all | solution.py:87
  73.6 14.2 %collective-permute-start = (f32[2,128,512]{2,1,0:T(8,128)}, f32[2,128,512]{2,1,0:T(8,128)S(1)}, u32[]{:S(2)}, u32[]{:S(2)}) collective-permute-start(f32[2,128,512]{2,1,0:T(8,128)} %bitcast.2), channel_id=1, source_target_pairs={{0,32},{32,64},{64,96},{96,128},{128,160},{160,192},{192,224},{224... | collective-permute-start | bytes 1572872 | tf_op jit(solution)/shard_map/ppermute | solution.py:18
  89.8 20.8 %collective-permute-done = f32[2,128,512]{2,1,0:T(8,128)S(1)} collective-permute-done((f32[2,128,512]{2,1,0:T(8,128)}, f32[2,128,512]{2,1,0:T(8,128)S(1)}, u32[]{:S(2)}, u32[]{:S(2)}) %collective-permute-start) | collective-permute-done | bytes 524320 | tf_op jit(solution)/shard_map/ppermute | solution.py:18
  113.6 3.8 collective-permute-start.2
  117.4 3.0 collective-permute-start.3
  120.5 18.5 %collective-permute-done.2 = f32[2,128,512]{2,1,0:T(8,128)S(1)} collective-permute-done((f32[2,128,512]{2,1,0:T(8,128)S(1)}, f32[2,128,512]{2,1,0:T(8,128)S(1)}, u32[]{:S(2)}, u32[]{:S(2)}) %collective-permute-start.2) | collective-permute-done | bytes 524320 | tf_op jit(solution)/shard_map/ppermute | solution.py:18
  142.1 2.9 fusion.30
  145.0 2.6 gather_fusion.1
  150.4 2.6 gather_fusion
  153.9 94.2 %all-gather.3.cloned.1.call-done = f32[16,128,512]{2,1,0:T(8,128)} async-done(((f32[1,128,512]{2,1,0:T(8,128)}), f32[16,128,512]{2,1,0:T(8,128)}) %all-gather.3.cloned.1.call-update) | async-done | bytes 4194320 | tf_op jit(solution)/shard_map/all_gather | solution.py:106
  248.1 2.6 reduce_sum.18
  252.5 283.2 %all-reduce.13.cloned.1.call-done = (f32[1024,128]{0,1:T(8,128)}, f32[128,128]{0,1:T(8,128)}) async-done(((f32[1024,128]{0,1:T(8,128)}, f32[128,128]{0,1:T(8,128)}), (f32[1024,128]{0,1:T(8,128)}, f32[128,128]{0,1:T(8,128)})) %all-reduce.13.cloned.1.call-update) | async-done | bytes 589840 | tf_op jit(solution)/shard_map/psum | solution.py:116
  537.8 11.7 %cholesky.44 = f32[128,128]{1,0:T(8,128)S(1)} custom-call(f32[128,128]{1,0:T(8,128)S(1)} %copy.26), custom_call_target="Cholesky" | custom-call | tf_op jit(solution)/shard_map/jit(cholesky)/cholesky | solution.py:118
  550.9 9.8 custom-call.11
  561.5 3.4 convolution_subtract_fusion.1
  568.6 2.6 gather_fusion.3
  572.1 95.4 %all-gather.5.cloned.1.call-done = f32[16,128,512]{2,1,0:T(8,128)} async-done(((f32[1,128,512]{2,1,0:T(8,128)}), f32[16,128,512]{2,1,0:T(8,128)}) %all-gather.5.cloned.1.call-update) | async-done | bytes 4194320 | tf_op jit(solution)/shard_map/all_gather | solution.py:106
  667.6 2.6 reduce_sum.19
  671.9 283.4 %all-reduce.11.cloned.1.call-done = (f32[1024,128]{0,1:T(8,128)}, f32[128,128]{1,0:T(8,128)}) async-done(((f32[1024,128]{0,1:T(8,128)}, f32[128,128]{1,0:T(8,128)}), (f32[1024,128]{0,1:T(8,128)}, f32[128,128]{1,0:T(8,128)})) %all-reduce.11.cloned.1.call-update) | async-done | bytes 589840 | tf_op jit(solution)/shard_map/psum | solution.py:116
  957.4 11.7 %cholesky.55 = f32[128,128]{1,0:T(8,128)S(1)} custom-call(f32[128,128]{1,0:T(8,128)S(1)} %fusion.47), custom_call_target="Cholesky" | custom-call | tf_op jit(solution)/shard_map/jit(cholesky)/cholesky | solution.py:118
  970.4 9.8 custom-call.13
  981.0 3.2 convolution_subtract_fusion
  (79 shorter events, 34.1 us)
Async XLA Ops:
  6.5 241.5 %all-gather.3.cloned.1.call-start = ((), (), s32[]{:S(2)}) async-start(), calls=%async_computation.1 | async-start | bytes 4456448 | tf_op jit(solution)/shard_map/all_gather | solution.py:106
  6.5 2.0 copy-start.3
  6.5 2.0 copy-start.4
  73.6 37.0 %collective-permute-start = (f32[2,128,512]{2,1,0:T(8,128)}, f32[2,128,512]{2,1,0:T(8,128)S(1)}, u32[]{:S(2)}, u32[]{:S(2)}) collective-permute-start(f32[2,128,512]{2,1,0:T(8,128)} %bitcast.2), channel_id=1, source_target_pairs={{0,32},{32,64},{64,96},{96,128},{128,160},{160,192},{192,224},{224... | collective-permute-start | bytes 1572872 | tf_op jit(solution)/shard_map/ppermute | solution.py:18
  87.8 23.3 %collective-permute-start.1 = (f32[2,128,512]{2,1,0:T(8,128)}, f32[2,128,512]{2,1,0:T(8,128)S(1)}, u32[]{:S(2)}, u32[]{:S(2)}) collective-permute-start(f32[2,128,512]{2,1,0:T(8,128)} %bitcast.4), channel_id=1, source_target_pairs={{32,0},{64,32},{96,64},{128,96},{160,128},{192,160},{224,192},{256... | collective-permute-start | bytes 1572872 | tf_op jit(solution)/shard_map/ppermute | solution.py:21
  113.5 6.8 copy-start.5
  113.6 25.3 %collective-permute-start.2 = (f32[2,128,512]{2,1,0:T(8,128)S(1)}, f32[2,128,512]{2,1,0:T(8,128)S(1)}, u32[]{:S(2)}, u32[]{:S(2)}) collective-permute-start(f32[2,128,512]{2,1,0:T(8,128)S(1)} %get-tuple-element.17), channel_id=1, source_target_pairs={{0,32},{32,64},{64,96},{96,128},{128,160},{160,192},{192,224},{224... | collective-permute-start | bytes 1572872 | tf_op jit(solution)/shard_map/ppermute | solution.py:18
  117.4 24.1 %collective-permute-start.3 = (f32[2,128,512]{2,1,0:T(8,128)S(1)}, f32[2,128,512]{2,1,0:T(8,128)S(1)}, u32[]{:S(2)}, u32[]{:S(2)}) collective-permute-start(f32[2,128,512]{2,1,0:T(8,128)S(1)} %get-tuple-element.16), channel_id=1, source_target_pairs={{32,0},{64,32},{96,64},{128,96},{160,128},{192,160},{224,192},{256... | collective-permute-start | bytes 1572872 | tf_op jit(solution)/shard_map/ppermute | solution.py:21
  145.0 3.5 copy-start
  148.4 387.2 %all-reduce.13.cloned.1.call-start = ((), (), s32[]{:S(2)}) async-start(), calls=%async_computation.4 | async-start | bytes 1179648 | tf_op jit(solution)/shard_map/psum | solution.py:116
  153.9 98.6 %copy-start.6 = (f32[2,128]{1,0:T(2,128)S(1)}, f32[2,128]{1,0:T(2,128)}, u32[]{:S(2)}) copy-start(f32[2,128]{1,0:T(2,128)} %param.14) | copy-start | bytes 3076
  252.2 415.3 %all-gather.5.cloned.1.call-start = ((), (), s32[]{:S(2)}) async-start(), calls=%async_computation.2 | async-start | bytes 4456448 | tf_op jit(solution)/shard_map/all_gather | solution.py:106
  535.7 25.8 %copy-start.1 = (f32[1024,128]{0,1:T(8,128)S(1)}, f32[1024,128]{0,1:T(8,128)}, u32[]{:S(2)}) copy-start(f32[1024,128]{0,1:T(8,128)} %get-tuple-element.10) | copy-start | bytes 1572868
  566.5 388.8 %all-reduce.11.cloned.1.call-start = ((), (), s32[]{:S(2)}) async-start(), calls=%async_computation.3 | async-start | bytes 1179648 | tf_op jit(solution)/shard_map/psum | solution.py:116
  955.3 25.8 %copy-start.2 = (f32[1024,128]{0,1:T(8,128)S(1)}, f32[1024,128]{0,1:T(8,128)}, u32[]{:S(2)}) copy-start(f32[1024,128]{0,1:T(8,128)} %get-tuple-element.6) | copy-start | bytes 1572868
Sparse Core Ops, SparseCore 0:
  148.6 99.4 all-gather.2
  252.4 283.2 all-reduce.12
  566.6 100.8 all-gather.4
  671.9 283.3 all-reduce.10
